TPU v7x, 128 devices: a whole 4x4x4 slice. The times are simulated.
128 devices in a mesh: tile: 32 (over z, x, core), group: 4 (over y).
Axes of the slice: x: 4, y: 4, z: 4, core: 2. Of those that a mesh axis runs over, the one named last changes fastest.
Arguments:
- latent: bfloat16 [8, 256, 40, 384], P('group', 'tile'), may hold values from -6 to 6
- conv_first: bfloat16 [3, 3, 3, 384, 384], replicated, may hold values from -0.0625 to 0.0625
- conv_second: bfloat16 [3, 3, 3, 384, 384], replicated, may hold values from -0.0625 to 0.0625
- time_weight: bfloat16 [3, 384, 768], replicated, may hold values from -0.1875 to 0.1875
- space_weight: bfloat16 [3, 3, 384, 192], replicated, may hold values from -0.109375 to 0.109375
Outputs:
- decoded: bfloat16 [16, 512, 80, 192], P('group', 'tile')
All inputs are finite; a program needn't handle non-finite values.
Results may differ from a plain program's by a relative error of at most 0.0085.
Values may be sent and summed in bfloat16 or wider, within the bound.
A program may use at most 128 MiB of HBM per device.

v0:
```python
import jax
import jax.numpy as jnp
from jax import lax
from jax.sharding import PartitionSpec as P


def shifted(value, axis, steps):
    count = lax.axis_size(axis)
    leading, last = (max(0, -steps), min(count, count - steps))
    return lax.ppermute(value, axis, [(source, source + steps) for source in range(leading, last)])


def with_halo(cells, sides, width):
    for axis, dim in sides:
        count = lax.axis_size(axis)
        ends = count - 1
        head = lax.slice_in_dim(cells, 0, width, axis=dim)
        tail = lax.slice_in_dim(cells, cells.shape[dim] - width, cells.shape[dim], axis=dim)
        cells = jnp.concatenate(
            [
                lax.ppermute(tail, axis, [(i, (i + 1) % count) for i in range(ends)]),
                cells,
                lax.ppermute(head, axis, [((i + 1) % count, i) for i in range(ends)]),
            ],
            axis=dim,
        )
    return cells


def rms_silu(value):
    value = value.astype(jnp.float32)
    value = value * lax.rsqrt(jnp.mean(value * value, axis=-1, keepdims=True) + 1e-06)
    return jax.nn.silu(value).astype(jnp.bfloat16)


def conv_cube(padded, weight):
    frames = padded.shape[0] - 2
    rows = padded.shape[1] - 2
    width = padded.shape[2]
    chans = padded.shape[3]
    outs = weight.shape[4]
    cols = jnp.pad(padded, ((0, 0), (0, 0), (1, 1), (0, 0)))
    wide = jnp.concatenate([cols[:, :, k : k + width] for k in range(3)], axis=-1)
    folded = weight.reshape(3, 3, 3 * chans, outs)
    total = jnp.zeros((frames * rows * width, outs), jnp.float32)
    for a in range(3):
        for b in range(3):
            piece = wide[a : a + frames, b : b + rows].reshape(-1, 3 * chans)
            total = total + jnp.dot(piece, folded[a, b], preferred_element_type=jnp.float32)
    return total.reshape(frames, rows, width, outs)


def time_double(padded, weight):
    frames = padded.shape[0] - 2
    rows, width, chans = (padded.shape[1], padded.shape[2], padded.shape[3])
    total = jnp.zeros((frames * rows * width, 2 * chans), jnp.float32)
    for a in range(3):
        total = total + jnp.dot(
            padded[a : a + frames].reshape(-1, chans), weight[a], preferred_element_type=jnp.float32
        )
    split = total.reshape(frames, rows, width, 2, chans)
    split = jnp.transpose(split, (0, 3, 1, 2, 4))
    return split.reshape(2 * frames, rows, width, chans).astype(jnp.bfloat16)


def space_conv(rows_ext, weight):
    rows = rows_ext.shape[1] - 2
    chans = rows_ext.shape[3]
    outs = weight.shape[3]
    upper = jnp.repeat(rows_ext, 2, axis=1)[:, 1:-1]
    upper = jnp.repeat(upper, 2, axis=2)
    width = upper.shape[2]
    cols = jnp.pad(upper, ((0, 0), (0, 0), (1, 1), (0, 0)))
    wide = jnp.concatenate([cols[:, :, k : k + width] for k in range(3)], axis=-1)
    folded = weight.reshape(3, 3 * chans, outs)
    count = upper.shape[0]
    total = jnp.zeros((count * 2 * rows * width, outs), jnp.float32)
    for b in range(3):
        total = total + jnp.dot(
            wide[:, b : b + 2 * rows].reshape(-1, 3 * chans),
            folded[b],
            preferred_element_type=jnp.float32,
        )
    return total.reshape(count, 2 * rows, width, outs).astype(jnp.bfloat16)


def local(latent, conv_first, conv_second, time_weight, space_weight):
    first = rms_silu(latent)
    earlier = shifted(first, "group", 1)
    extended = jnp.concatenate([earlier, first], axis=0)
    padded = with_halo(extended, (("tile", 1),), 1)
    second = rms_silu(conv_cube(padded, conv_first))
    earlier = shifted(second, "group", 1)
    extended = jnp.concatenate([earlier, second], axis=0)
    padded = with_halo(extended, (("tile", 1),), 1)
    mixed = (latent.astype(jnp.float32) + conv_cube(padded, conv_second)).astype(jnp.bfloat16)
    earlier = shifted(mixed, "group", 1)
    upframes = time_double(jnp.concatenate([earlier, mixed], axis=0), time_weight)
    rows_ext = with_halo(upframes, (("tile", 1),), 1)
    return space_conv(rows_ext, space_weight)


def solution(mesh):
    in_specs = (P("group", "tile", None, None), P(), P(), P(), P())
    out_specs = P("group", "tile", None, None)
    return jax.shard_map(local, mesh=mesh, in_specs=in_specs, out_specs=out_specs, check_vma=False)
```

profile of v0, /device:TPU:23, one launch (start us, length us, event | category | flops | bytes accessed | tf_op | source)
XLA Modules:
  0.0 164.4 jit_solution(18426764180672820799)
XLA Ops:
  0.0 1.2 fusion.32
  1.2 1.4 fusion.31
  2.6 2.9 %collective-permute-start = (bf16[2,8,40,384]{3,2,1,0:T(8,128)(2,1)S(1)}, bf16[2,8,40,384]{3,2,1,0:T(8,128)(2,1)S(1)}, u32[]{:S(2)}, u32[]{:S(2)}) collective-permute-start(bf16[2,8,40,384]{3,2,1,0:T(8,128)(2,1)S(1)} %fusion.31), channel_id=1, source_target_pairs={{0,1},{1,2},{2,3},{4,5},{5,6},{6,7},{8,9},{9,10},{10,11},{12,13},{... | collective-permute-start | bytes 1474568 | tf_op jit(solution)/shard_map/ppermute | solution.py:10
  5.5 11.1 %collective-permute-done = bf16[2,8,40,384]{3,2,1,0:T(8,128)(2,1)S(1)} collective-permute-done((bf16[2,8,40,384]{3,2,1,0:T(8,128)(2,1)S(1)}, bf16[2,8,40,384]{3,2,1,0:T(8,128)(2,1)S(1)}, u32[]{:S(2)}, u32[]{:S(2)}) %collective-permute-start) | collective-permute-done | bytes 491552 | tf_op jit(solution)/shard_map/ppermute | solution.py:10
  16.6 4.9 %collective-permute-start.1 = (bf16[4,1,40,384]{3,2,1,0:T(8,128)(2,1)S(1)}, bf16[4,1,40,384]{3,2,1,0:T(8,128)(2,1)S(1)}, u32[]{:S(2)}, u32[]{:S(2)}) collective-permute-start(bf16[4,1,40,384]{3,2,1,0:T(8,128)(2,1)S(1)} %get-tuple-element.39), channel_id=1, source_target_pairs={{0,4},{4,8},{8,12},{12,16},{16,20},{20,24},{24,28},{28,32},{32,36}... | collective-permute-start | bytes 368648 | tf_op jit(solution)/shard_map/ppermute | solution.py:21
  21.5 1.9 %collective-permute-start.2 = (bf16[4,1,40,384]{3,2,1,0:T(8,128)(2,1)S(1)}, bf16[4,1,40,384]{3,2,1,0:T(8,128)(2,1)S(1)}, u32[]{:S(2)}, u32[]{:S(2)}) collective-permute-start(bf16[4,1,40,384]{3,2,1,0:T(8,128)(2,1)S(1)} %get-tuple-element.40), channel_id=1, source_target_pairs={{4,0},{8,4},{12,8},{16,12},{20,16},{24,20},{28,24},{32,28},{36,32}... | collective-permute-start | bytes 368648 | tf_op jit(solution)/shard_map/ppermute | solution.py:23
  23.4 6.4 %collective-permute-done.2 = bf16[4,1,40,384]{3,2,1,0:T(8,128)(2,1)S(1)} collective-permute-done((bf16[4,1,40,384]{3,2,1,0:T(8,128)(2,1)S(1)}, bf16[4,1,40,384]{3,2,1,0:T(8,128)(2,1)S(1)}, u32[]{:S(2)}, u32[]{:S(2)}) %collective-permute-start.2) | collective-permute-done | bytes 122912 | tf_op jit(solution)/shard_map/ppermute | solution.py:23
  29.8 0.8 fusion.9
  30.6 0.7 fusion.62
  31.3 1.0 pad_maximum_fusion.1
  32.4 1.7 %fusion.60 = (bf16[2,8,40,1152]{3,2,1,0:T(8,128)(2,1)S(1)}, bf16[2,8,40,1152]{3,2,1,0:T(8,128)(2,1)S(1)}, bf16[2,8,40,1152]{3,2,1,0:T(8,128)(2,1)S(1)}, bf16[2,8...) fusion(bf16[4,10,40,1152]{3,2,1,0:T(8,128)(2,1)S(1)} %pad_maxim, ...), kind=kLoop, calls=%fused_computation.105 | loop fusion | bytes 26542080 | tf_op jit(solution)/shard_map/slice | solution.py:48
  34.2 0.7 slice-done.1
  34.9 1.0 fusion.42
  35.9 1.0 fusion.43
  36.8 1.0 fusion.44
  37.8 1.0 fusion.45
  38.8 1.0 fusion.46
  39.7 1.0 fusion.47
  40.7 1.0 fusion.48
  41.6 1.0 fusion.49
  42.6 2.5 %multiply_reduce_fusion = (f32[640]{0:T(1024)S(1)}, f32[640,384]{1,0:T(8,128)S(1)}) fusion(f32[640,384]{1,0:T(8,128)S(1)} %fusion.42, f32[640,384]{1,0:T(8,128)S(1)} %fusion.43, f32[640,384]{1,0:T(8,128)S(1)} %fusion.44, f32[640,384]{1,0:T(8,128)S(1)} %fusion.45, f32[640,384]{1,0:T(8,128)S(1)} %fusion.46, f32[640,384]{1,0:T(8,128)S(1)} %fusion.47, ...), kind=kOutput, calls=%fused_computation.53 | convolution fusion | flops 568688000 | bytes 11209216 | tf_op jit(solution)/shard_map/dot_general | solution.py:49
  45.2 0.3 multiply_convert_fusion
  45.6 2.9 %collective-permute-start.3 = (bf16[2,8,40,384]{3,2,1,0:T(8,128)(2,1)S(1)}, bf16[2,8,40,384]{3,2,1,0:T(8,128)(2,1)S(1)}, u32[]{:S(2)}, u32[]{:S(2)}) collective-permute-start(bf16[2,8,40,384]{3,2,1,0:T(8,128)(2,1)S(1)} %multiply_convert_fusion), channel_id=1, source_target_pairs={{0,1},{1,2},{2,3},{4,5},{5,6},{6,7},{8,9},{9,10},{10,11},{12,13},{... | collective-permute-start | bytes 1474568 | tf_op jit(solution)/shard_map/ppermute | solution.py:10
  48.5 8.7 %collective-permute-done.3 = bf16[2,8,40,384]{3,2,1,0:T(8,128)(2,1)S(1)} collective-permute-done((bf16[2,8,40,384]{3,2,1,0:T(8,128)(2,1)S(1)}, bf16[2,8,40,384]{3,2,1,0:T(8,128)(2,1)S(1)}, u32[]{:S(2)}, u32[]{:S(2)}) %collective-permute-start.3) | collective-permute-done | bytes 491552 | tf_op jit(solution)/shard_map/ppermute | solution.py:10
  57.3 4.8 %collective-permute-start.4 = (bf16[4,1,40,384]{3,2,1,0:T(8,128)(2,1)S(1)}, bf16[4,1,40,384]{3,2,1,0:T(8,128)(2,1)S(1)}, u32[]{:S(2)}, u32[]{:S(2)}) collective-permute-start(bf16[4,1,40,384]{3,2,1,0:T(8,128)(2,1)S(1)} %get-tuple-element.37), channel_id=1, source_target_pairs={{0,4},{4,8},{8,12},{12,16},{16,20},{20,24},{24,28},{28,32},{32,36}... | collective-permute-start | bytes 368648 | tf_op jit(solution)/shard_map/ppermute | solution.py:21
  62.1 2.1 %collective-permute-start.5 = (bf16[4,1,40,384]{3,2,1,0:T(8,128)(2,1)S(1)}, bf16[4,1,40,384]{3,2,1,0:T(8,128)(2,1)S(1)}, u32[]{:S(2)}, u32[]{:S(2)}) collective-permute-start(bf16[4,1,40,384]{3,2,1,0:T(8,128)(2,1)S(1)} %get-tuple-element.38), channel_id=1, source_target_pairs={{4,0},{8,4},{12,8},{16,12},{20,16},{24,20},{28,24},{32,28},{36,32}... | collective-permute-start | bytes 368648 | tf_op jit(solution)/shard_map/ppermute | solution.py:23
  64.2 6.2 %collective-permute-done.5 = bf16[4,1,40,384]{3,2,1,0:T(8,128)(2,1)S(1)} collective-permute-done((bf16[4,1,40,384]{3,2,1,0:T(8,128)(2,1)S(1)}, bf16[4,1,40,384]{3,2,1,0:T(8,128)(2,1)S(1)}, u32[]{:S(2)}, u32[]{:S(2)}) %collective-permute-start.5) | collective-permute-done | bytes 122912 | tf_op jit(solution)/shard_map/ppermute | solution.py:23
  70.4 0.8 select_maximum_fusion
  71.1 0.7 fusion.61
  71.9 1.0 pad_maximum_fusion.2
  73.0 1.7 %fusion.59 = (bf16[2,8,40,1152]{3,2,1,0:T(8,128)(2,1)S(1)}, bf16[2,8,40,1152]{3,2,1,0:T(8,128)(2,1)S(1)}, bf16[2,8,40,1152]{3,2,1,0:T(8,128)(2,1)S(1)}, bf16[2,8...) fusion(bf16[4,10,40,1152]{3,2,1,0:T(8,128)(2,1)S(1)} %pad_maxim, ...), kind=kLoop, calls=%fused_computation.104 | loop fusion | bytes 26542080 | tf_op jit(solution)/shard_map/slice | solution.py:48
  74.7 0.7 slice-done.3
  75.5 1.0 fusion.34
  76.4 1.0 fusion.35
  77.4 1.0 fusion.36
  78.3 1.0 fusion.37
  79.3 1.0 fusion.38
  80.3 1.0 fusion.39
  81.2 1.0 fusion.40
  82.2 1.0 fusion.41
  83.2 1.2 fusion.21
  84.5 3.0 %collective-permute-start.6 = (bf16[2,8,40,384]{3,2,1,0:T(8,128)(2,1)S(1)}, bf16[2,8,40,384]{3,2,1,0:T(8,128)(2,1)S(1)}, u32[]{:S(2)}, u32[]{:S(2)}) collective-permute-start(bf16[2,8,40,384]{3,2,1,0:T(8,128)(2,1)S(1)} %fusion.33), channel_id=1, source_target_pairs={{0,1},{1,2},{2,3},{4,5},{5,6},{6,7},{8,9},{9,10},{10,11},{12,13},{... | collective-permute-start | bytes 1474568 | tf_op jit(solution)/shard_map/ppermute | solution.py:10
  87.6 0.7 fusion.50
  88.2 6.6 %collective-permute-done.6 = bf16[2,8,40,384]{3,2,1,0:T(8,128)(2,1)S(1)} collective-permute-done((bf16[2,8,40,384]{3,2,1,0:T(8,128)(2,1)S(1)}, bf16[2,8,40,384]{3,2,1,0:T(8,128)(2,1)S(1)}, u32[]{:S(2)}, u32[]{:S(2)}) %collective-permute-start.6) | collective-permute-done | bytes 491552 | tf_op jit(solution)/shard_map/ppermute | solution.py:10
  94.9 0.7 fusion.52
  95.6 0.7 add_convert_fusion
  96.3 0.2 convert_element_type.41
  96.7 4.9 %collective-permute-start.7 = (bf16[4,1,40,384]{3,2,1,0:T(8,128)(2,1)S(1)}, bf16[4,1,40,384]{3,2,1,0:T(8,128)(2,1)S(1)}, u32[]{:S(2)}, u32[]{:S(2)}) collective-permute-start(bf16[4,1,40,384]{3,2,1,0:T(8,128)(2,1)S(1)} %get-tuple-element.35), channel_id=1, source_target_pairs={{0,4},{4,8},{8,12},{12,16},{16,20},{20,24},{24,28},{28,32},{32,36}... | collective-permute-start | bytes 368648 | tf_op jit(solution)/shard_map/ppermute | solution.py:21
  101.6 2.1 %collective-permute-start.8 = (bf16[4,1,40,384]{3,2,1,0:T(8,128)(2,1)S(1)}, bf16[4,1,40,384]{3,2,1,0:T(8,128)(2,1)S(1)}, u32[]{:S(2)}, u32[]{:S(2)}) collective-permute-start(bf16[4,1,40,384]{3,2,1,0:T(8,128)(2,1)S(1)} %get-tuple-element.36), channel_id=1, source_target_pairs={{4,0},{8,4},{12,8},{16,12},{20,16},{24,20},{28,24},{32,28},{36,32}... | collective-permute-start | bytes 368648 | tf_op jit(solution)/shard_map/ppermute | solution.py:23
  103.9 0.4 copy.8
  104.3 0.4 copy.9
  104.8 0.4 copy.10
  105.3 4.6 %collective-permute-done.8 = bf16[4,1,40,384]{3,2,1,0:T(8,128)(2,1)S(1)} collective-permute-done((bf16[4,1,40,384]{3,2,1,0:T(8,128)(2,1)S(1)}, bf16[4,1,40,384]{3,2,1,0:T(8,128)(2,1)S(1)}, u32[]{:S(2)}, u32[]{:S(2)}) %collective-permute-start.8) | collective-permute-done | bytes 122912 | tf_op jit(solution)/shard_map/ppermute | solution.py:23
  110.3 0.2 slice.284
  110.5 3.7 %broadcast_in_dim.9 = bf16[4,18,40,2,384]{4,3,2,1,0:T(2,128)(2,1)} broadcast(bf16[4,18,40,384]{3,2,1,0:T(8,128)(2,1)S(1)} %slice.284), dimensions={0,1,2,4} | broadcast | bytes 6635520 | tf_op jit(solution)/shard_map/broadcast_in_dim | solution.py:71
  114.2 10.1 %reshape.154 = bf16[4,18,80,384]{3,2,1,0:T(8,128)(2,1)} reshape(bf16[4,18,40,2,384]{4,3,2,1,0:T(2,128)(2,1)} %broadcast_in_dim.9) | data formatting | bytes 8847360 | tf_op jit(solution)/shard_map/reshape | solution.py:71
  124.3 8.1 %pad_slice_fusion.1 = (bf16[4,18,80,384]{3,2,1,0:T(8,128)(2,1)S(1)}, bf16[4,18,80,384]{3,2,1,0:T(8,128)(2,1)S(1)}) fusion(bf16[4,18,80,384]{3,2,1,0:T(8,128)(2,1)} %reshape.154), kind=kLoop, calls=%fused_computation.5 | loop fusion | bytes 13271040 | tf_op jit(solution)/shard_map/slice | solution.py:74
  132.4 1.3 pad_maximum_fusion
  133.7 9.4 %fusion.58 = (bf16[4,16,80,1152]{3,2,1,0:T(8,128)(2,1)S(1)}, bf16[4,16,80,1152]{3,2,1,0:T(8,128)(2,1)}, bf16[4,16,80,1152]{3,2,1,0:T(8,128)(2,1)}) fusion(bf16[4,18,80,1152]{3,2,1,0:T(8,128)(2,1)S(1)} %pad_maximum_fusion), kind=kLoop, calls=%fused_computation.103 | loop fusion | bytes 70778880 | tf_op jit(solution)/shard_map/slice | solution.py:80
  143.1 7.0 %fusion.65 = f32[5120,192]{0,1:T(8,128)S(1)} fusion(bf16[5120,1152]{1,0:T(8,128)(2,1)} %bitcast.142, bf16[1152,192]{0,1:T(8,128)(2,1)S(1)} %bitcast.156), kind=kOutput, calls=%fused_computation.110 | convolution fusion | flops 2264924160 | bytes 16171008 | tf_op jit(solution)/shard_map/dot_general | solution.py:79
  150.1 0.7 copy-done
  150.8 4.1 %convolution_add_fusion.1 = f32[5120,192]{0,1:T(8,128)S(1)} fusion(f32[5120,192]{0,1:T(8,128)S(1)} %fusion.65, bf16[5120,1152]{1,0:T(8,128)(2,1)S(1)} %bitcast.141, bf16[1152,192]{0,1:T(8,128)(2,1)S(1)} %bitcast.157), kind=kOutput, calls=%fused_computation.3 | convolution fusion | flops 2265907200 | bytes 20103168 | tf_op jit(solution)/shard_map/dot_general | solution.py:79
  154.9 5.3 %fusion = bf16[5120,192]{0,1:T(8,128)(2,1)} fusion(f32[5120,192]{0,1:T(8,128)S(1)} %convolution_add_fusion.1, bf16[5120,1152]{1,0:T(8,128)(2,1)S(1)} %bitcast.140, bf16[1152,192]{0,1:T(8,128)(2,1)S(1)} %bitcast.158), kind=kOutput, calls=%fused_computation.2 | convolution fusion | flops 2266890240 | bytes 18137088 | tf_op jit(solution)/shard_map/dot_general | solution.py:79
  160.2 4.2 %copy.11 = bf16[5120,192]{1,0:T(8,128)(2,1)} copy(bf16[5120,192]{0,1:T(8,128)(2,1)} %fusion) | data formatting | bytes 3932160 | tf_op jit(solution)/shard_map/convert_element_type | solution.py:84
  (35 shorter events, 1.2 us)
Async XLA Ops:
  2.6 14.0 %collective-permute-start = (bf16[2,8,40,384]{3,2,1,0:T(8,128)(2,1)S(1)}, bf16[2,8,40,384]{3,2,1,0:T(8,128)(2,1)S(1)}, u32[]{:S(2)}, u32[]{:S(2)}) collective-permute-start(bf16[2,8,40,384]{3,2,1,0:T(8,128)(2,1)S(1)} %fusion.31), channel_id=1, source_target_pairs={{0,1},{1,2},{2,3},{4,5},{5,6},{6,7},{8,9},{9,10},{10,11},{12,13},{... | collective-permute-start | bytes 1474568 | tf_op jit(solution)/shard_map/ppermute | solution.py:10
  16.6 6.8 %collective-permute-start.1 = (bf16[4,1,40,384]{3,2,1,0:T(8,128)(2,1)S(1)}, bf16[4,1,40,384]{3,2,1,0:T(8,128)(2,1)S(1)}, u32[]{:S(2)}, u32[]{:S(2)}) collective-permute-start(bf16[4,1,40,384]{3,2,1,0:T(8,128)(2,1)S(1)} %get-tuple-element.39), channel_id=1, source_target_pairs={{0,4},{4,8},{8,12},{12,16},{16,20},{20,24},{24,28},{28,32},{32,36}... | collective-permute-start | bytes 368648 | tf_op jit(solution)/shard_map/ppermute | solution.py:21
  21.5 8.3 %collective-permute-start.2 = (bf16[4,1,40,384]{3,2,1,0:T(8,128)(2,1)S(1)}, bf16[4,1,40,384]{3,2,1,0:T(8,128)(2,1)S(1)}, u32[]{:S(2)}, u32[]{:S(2)}) collective-permute-start(bf16[4,1,40,384]{3,2,1,0:T(8,128)(2,1)S(1)} %get-tuple-element.40), channel_id=1, source_target_pairs={{4,0},{8,4},{12,8},{16,12},{20,16},{24,20},{28,24},{32,28},{36,32}... | collective-permute-start | bytes 368648 | tf_op jit(solution)/shard_map/ppermute | solution.py:23
  31.3 2.8 %slice-start = ((s8[7962624]{0:T(1024)(128)(4,1)}), s8[4194304]{0:T(1024)(128)(4,1)S(1)}, s32[]{:S(2)}) async-start(s8[7962624]{0:T(1024)(128)(4,1)} %bitcast.176), calls=%async_computation | async-start | bytes 8388608
  32.4 2.5 %slice-start.1 = ((s8[7962624]{0:T(1024)(128)(4,1)}), s8[3768320]{0:T(1024)(128)(4,1)S(1)}, s32[]{:S(2)}) async-start(s8[7962624]{0:T(1024)(128)(4,1)} %bitcast.176), calls=%async_computation.1 | async-start | bytes 7536640
  45.6 11.6 %collective-permute-start.3 = (bf16[2,8,40,384]{3,2,1,0:T(8,128)(2,1)S(1)}, bf16[2,8,40,384]{3,2,1,0:T(8,128)(2,1)S(1)}, u32[]{:S(2)}, u32[]{:S(2)}) collective-permute-start(bf16[2,8,40,384]{3,2,1,0:T(8,128)(2,1)S(1)} %multiply_convert_fusion), channel_id=1, source_target_pairs={{0,1},{1,2},{2,3},{4,5},{5,6},{6,7},{8,9},{9,10},{10,11},{12,13},{... | collective-permute-start | bytes 1474568 | tf_op jit(solution)/shard_map/ppermute | solution.py:10
  57.3 6.9 %collective-permute-start.4 = (bf16[4,1,40,384]{3,2,1,0:T(8,128)(2,1)S(1)}, bf16[4,1,40,384]{3,2,1,0:T(8,128)(2,1)S(1)}, u32[]{:S(2)}, u32[]{:S(2)}) collective-permute-start(bf16[4,1,40,384]{3,2,1,0:T(8,128)(2,1)S(1)} %get-tuple-element.37), channel_id=1, source_target_pairs={{0,4},{4,8},{8,12},{12,16},{16,20},{20,24},{24,28},{28,32},{32,36}... | collective-permute-start | bytes 368648 | tf_op jit(solution)/shard_map/ppermute | solution.py:21
  62.1 8.3 %collective-permute-start.5 = (bf16[4,1,40,384]{3,2,1,0:T(8,128)(2,1)S(1)}, bf16[4,1,40,384]{3,2,1,0:T(8,128)(2,1)S(1)}, u32[]{:S(2)}, u32[]{:S(2)}) collective-permute-start(bf16[4,1,40,384]{3,2,1,0:T(8,128)(2,1)S(1)} %get-tuple-element.38), channel_id=1, source_target_pairs={{4,0},{8,4},{12,8},{16,12},{20,16},{24,20},{28,24},{32,28},{36,32}... | collective-permute-start | bytes 368648 | tf_op jit(solution)/shard_map/ppermute | solution.py:23
  71.9 2.8 %slice-start.2 = ((s8[7962624]{0:T(1024)(128)(4,1)}), s8[4194304]{0:T(1024)(128)(4,1)S(1)}, s32[]{:S(2)}) async-start(s8[7962624]{0:T(1024)(128)(4,1)} %bitcast.186), calls=%async_computation.2 | async-start | bytes 8388608
  72.9 2.5 %slice-start.3 = ((s8[7962624]{0:T(1024)(128)(4,1)}), s8[3768320]{0:T(1024)(128)(4,1)S(1)}, s32[]{:S(2)}) async-start(s8[7962624]{0:T(1024)(128)(4,1)} %bitcast.186), calls=%async_computation.3 | async-start | bytes 7536640
  83.2 1.2 copy-start.2
  84.4 3.2 %copy-start.3 = (bf16[3,384,768]{2,1,0:T(8,128)(2,1)S(1)}, bf16[3,384,768]{2,1,0:T(8,128)(2,1)}, u32[]{:S(2)}) copy-start(bf16[3,384,768]{2,1,0:T(8,128)(2,1)} %param.8) | copy-start | bytes 5308420
  84.5 10.3 %collective-permute-start.6 = (bf16[2,8,40,384]{3,2,1,0:T(8,128)(2,1)S(1)}, bf16[2,8,40,384]{3,2,1,0:T(8,128)(2,1)S(1)}, u32[]{:S(2)}, u32[]{:S(2)}) collective-permute-start(bf16[2,8,40,384]{3,2,1,0:T(8,128)(2,1)S(1)} %fusion.33), channel_id=1, source_target_pairs={{0,1},{1,2},{2,3},{4,5},{5,6},{6,7},{8,9},{9,10},{10,11},{12,13},{... | collective-permute-start | bytes 1474568 | tf_op jit(solution)/shard_map/ppermute | solution.py:10
  96.3 7.5 %copy-start.4 = (bf16[3,3,384,192]{2,3,1,0:T(8,128)(2,1)S(1)}, bf16[3,3,384,192]{2,3,1,0:T(8,128)(2,1)}, u32[]{:S(2)}) copy-start(bf16[3,3,384,192]{2,3,1,0:T(8,128)(2,1)} %param.9) | copy-start | bytes 3981316
  96.7 8.6 %collective-permute-start.7 = (bf16[4,1,40,384]{3,2,1,0:T(8,128)(2,1)S(1)}, bf16[4,1,40,384]{3,2,1,0:T(8,128)(2,1)S(1)}, u32[]{:S(2)}, u32[]{:S(2)}) collective-permute-start(bf16[4,1,40,384]{3,2,1,0:T(8,128)(2,1)S(1)} %get-tuple-element.35), channel_id=1, source_target_pairs={{0,4},{4,8},{8,12},{12,16},{16,20},{20,24},{24,28},{28,32},{32,36}... | collective-permute-start | bytes 368648 | tf_op jit(solution)/shard_map/ppermute | solution.py:21
  101.6 8.3 %collective-permute-start.8 = (bf16[4,1,40,384]{3,2,1,0:T(8,128)(2,1)S(1)}, bf16[4,1,40,384]{3,2,1,0:T(8,128)(2,1)S(1)}, u32[]{:S(2)}, u32[]{:S(2)}) collective-permute-start(bf16[4,1,40,384]{3,2,1,0:T(8,128)(2,1)S(1)} %get-tuple-element.36), channel_id=1, source_target_pairs={{4,0},{8,4},{12,8},{16,12},{20,16},{24,20},{28,24},{32,28},{36,32}... | collective-permute-start | bytes 368648 | tf_op jit(solution)/shard_map/ppermute | solution.py:23
  124.3 8.1 %copy-start.1 = (bf16[4,18,80,384]{3,2,1,0:T(8,128)(2,1)S(1)}, bf16[4,18,80,384]{3,2,1,0:T(8,128)(2,1)}, u32[]{:S(2)}) copy-start(bf16[4,18,80,384]{3,2,1,0:T(8,128)(2,1)} %reshape.154) | copy-start | bytes 13271044
  143.1 7.7 %copy-start = (bf16[4,16,80,1152]{3,2,1,0:T(8,128)(2,1)S(1)}, bf16[4,16,80,1152]{3,2,1,0:T(8,128)(2,1)}, u32[]{:S(2)}) copy-start(bf16[4,16,80,1152]{3,2,1,0:T(8,128)(2,1)} %get-tuple-element.6) | copy-start | bytes 35389444
where the time goes:
time: 165 us; the launch traced here: 164 us
  local copies, waits for them, and re-layouts  45 us (27%)
  waiting for transfers between devices  43.6 us (26%)
  matrix products  37.4 us (23%)
  starting transfers between devices  29.6 us (18%)
  other arithmetic  8.2 us (5%)
    ppermute x3, waiting for transfers between devices, shifted(): lax.ppermute(value, axis, [(source, source + steps) for source in range(l...  26.4 us
    dot_general x18, matrix products, conv_cube(): jnp.dot(piece, folded[a, b], preferred_element_type=jnp.float32)  19 us
    ppermute x3, waiting for transfers between devices, with_halo(): lax.ppermute(head, axis, [((i + 1) % count, i) for i in range(ends)])  17.2 us
    dot_general x3, matrix products, space_conv(): jnp.dot(wide[:, b:b + 2 * rows].reshape(-1, 3 * chans), folded[b], prefer...  16.4 us
    ppermute x3, starting transfers between devices, with_halo(): lax.ppermute(tail, axis, [(i, (i + 1) % count) for i in range(ends)])  14.6 us
    reshape x1, local copies, waits for them, and re-layouts, space_conv(): upper = jnp.repeat(upper, 2, axis=2)  10.1 us
    slice x1, local copies, waits for them, and re-layouts, space_conv(): wide[:, b:b + 2 * rows].reshape(-1, 3 * chans)  9.38 us
    ppermute x3, starting transfers between devices, shifted(): lax.ppermute(value, axis, [(source, source + steps) for source in range(l...  8.86 us
  transfers between devices with their start and end apart: 9, of which 6 were waited for; matrix products, arithmetic and copies ran while one was open for 1% of the time, Pallas kernels for 0%

commit v1 on v0

v1 whole, which is shorter than its diff:
```python
import functools

import jax
import jax.numpy as jnp
from jax import lax
from jax.experimental import pallas as pl
from jax.experimental.pallas import tpu as pltpu
from jax.sharding import PartitionSpec as P

MESH = pl.DeviceIdType.MESH
BF = jnp.bfloat16
F32 = jnp.float32

OUTER = ((0, 2), (6, 2))
INNER = ((2, 4),)
OUTER_SENDS = ((1, 1), (8, 1), (2, 1), (7, 1))
INNER_SENDS = ((3, 1), (6, 1), (4, 2))
SENDS = OUTER_SENDS + INNER_SENDS
NY = len(SENDS)


def rms_silu(v):
    v = v * lax.rsqrt(jnp.mean(v * v, axis=-1, keepdims=True) + 1e-06)
    return v / (1.0 + jnp.exp(-v))


def shift_down(v):
    at = lax.broadcasted_iota(jnp.int32, v.shape, 0)
    return jnp.where(at == 0, 0.0, pltpu.roll(v, 1, 0))


def shift_up(v):
    at = lax.broadcasted_iota(jnp.int32, v.shape, 0)
    return jnp.where(at == v.shape[0] - 1, 0.0, pltpu.roll(v, v.shape[0] - 1, 0))


def kernel(
    tiles, groups,
    latent, conv_first, conv_second, time_weight, space_weight, out,
    lat, X, W, wt, ws, wsp, Y, U, Z, T, O,
    lat_sem, w_sem, wt_sem, ws_sem, out_sem, y_send, y_recv, t_send, t_recv,
):
    t = lax.axis_index("tile")
    g = lax.axis_index("group")
    wide = lat.shape[2]
    ch = lat.shape[3]
    has_up, has_down = t > 0, t < tiles - 1
    has_prev, has_next = g > 0, g < groups - 1
    up = (lax.rem(t + tiles - 1, tiles), g)
    down = (lax.rem(t + 1, tiles), g)
    prev = (t, lax.rem(g + groups - 1, groups))
    after = (t, lax.rem(g + 1, groups))

    barrier = pltpu.get_barrier_semaphore()
    for other in (up, down, prev, after):
        pl.semaphore_signal(barrier, inc=1, device_id=other, device_id_type=MESH)

    lat_copy = pltpu.make_async_copy(latent, lat, lat_sem)
    lat_copy.start()
    w_copies = []
    for s, src in ((0, conv_first), (1, conv_second)):
        for a in (2, 1, 0):
            for b in range(3):
                w_copies.append(pltpu.make_async_copy(src.at[a, b], W.at[s, a, b], w_sem.at[s, a, b]))
    for c in w_copies[:9]:
        c.start()
    wt_copy = pltpu.make_async_copy(time_weight, wt, wt_sem)
    ws_copy = pltpu.make_async_copy(space_weight, ws, ws_sem)
    ws_copy.start()
    for c in w_copies[9:]:
        c.start()
    wt_copy.start()

    def wait_w(s, a):
        for b in range(3):
            pltpu.make_async_copy(conv_first.at[a, b], W.at[s, a, b], w_sem.at[s, a, b]).wait()

    @pl.when(jnp.logical_not(has_prev))
    def _():
        for s in range(3):
            for f in range(2):
                X[s, f] = jnp.zeros(X.shape[2:], BF)

    @pl.when(jnp.logical_not(has_up))
    def _():
        for s in range(3):
            X[s, :, 0] = jnp.zeros((4,) + X.shape[3:], BF)

    @pl.when(jnp.logical_not(has_down))
    def _():
        for s in range(3):
            X[s, :, 9] = jnp.zeros((4,) + X.shape[3:], BF)

    lat_copy.wait()

    def act_own(i, c):
        f, r = i // 8, i % 8
        X[0, 2 + f, 1 + r] = rms_silu(lat[f, r].astype(F32)).astype(BF)
        return c

    lax.fori_loop(0, 16, act_own, 0)

    pl.semaphore_wait(barrier, 4)

    def y_copy(s, k):
        row, count = SENDS[k]
        return pltpu.make_async_remote_copy(
            src_ref=X.at[s, pl.ds(2, 2), pl.ds(row, count)],
            dst_ref=X.at[s, pl.ds(0, 2), pl.ds(row, count)],
            send_sem=y_send.at[s, k],
            recv_sem=y_recv.at[s, k],
            device_id=after,
            device_id_type=MESH,
        )

    def t_copy(s, k):
        frame = 2 if k < 2 else 0
        row, slot, other = (1, 9, up) if k % 2 == 0 else (8, 0, down)
        return pltpu.make_async_remote_copy(
            src_ref=X.at[s, pl.ds(frame, 2), row],
            dst_ref=X.at[s, pl.ds(frame, 2), slot],
            send_sem=t_send.at[s, k],
            recv_sem=t_recv.at[s, k],
            device_id=other,
            device_id_type=MESH,
        )

    def send_outer(s):
        @pl.when(has_next)
        def _():
            y_copy(s, 0).start()
            y_copy(s, 1).start()

        @pl.when(has_up)
        def _():
            t_copy(s, 0).start()

        @pl.when(has_down)
        def _():
            t_copy(s, 1).start()

        @pl.when(has_next)
        def _():
            y_copy(s, 2).start()
            y_copy(s, 3).start()

    def send_inner(s):
        @pl.when(has_next)
        def _():
            for k in range(len(OUTER_SENDS), NY):
                y_copy(s, k).start()

    def wait_own_halo(s):
        @pl.when(has_down)
        def _():
            t_copy(s, 0).wait_recv()

        @pl.when(has_up)
        def _():
            t_copy(s, 1).wait_recv()

    def forward(s):
        @pl.when(has_prev)
        def _():
            y_copy(s, 0).wait_recv()

            @pl.when(has_up)
            def _():
                t_copy(s, 2).start()

            y_copy(s, 1).wait_recv()

            @pl.when(has_down)
            def _():
                t_copy(s, 3).start()

    def wait_outer(s):
        @pl.when(has_prev)
        def _():
            for k in range(2, NY - 1):
                y_copy(s, k).wait_recv()

            @pl.when(has_down)
            def _():
                t_copy(s, 2).wait_recv()

            @pl.when(has_up)
            def _():
                t_copy(s, 3).wait_recv()

    def wait_inner(s):
        @pl.when(has_prev)
        def _():
            y_copy(s, NY - 1).wait_recv()

    def taps(s, a, frames, spans, first):
        parts = []
        for b in range(3):
            rows = []
            for f in frames:
                for r, n in spans:
                    rows.append(X[s, f + a, r + b : r + b + n].reshape(n * wide, ch))
            parts.append(jnp.concatenate(rows, axis=0))
        lhs = jnp.concatenate(parts, axis=1)
        rhs = jnp.concatenate(
            [jnp.concatenate([W[s, a, b, e] for e in range(3)], axis=1) for b in range(3)], axis=0
        )
        d = jnp.dot(lhs, rhs, preferred_element_type=F32)
        at = 0
        for f in frames:
            for r, n in spans:
                piece = d[at : at + n * wide].reshape(n, wide, 3 * ch)
                if first:
                    Y[f, r : r + n] = piece
                else:
                    Y[f, r : r + n] += piece
                at += n * wide

    def own(s, spans):
        taps(s, 2, (0, 1), spans, True)
        taps(s, 1, (1,), spans, False)

    def earlier(s, spans):
        taps(s, 1, (0,), spans, False)
        taps(s, 0, (0, 1), spans, False)

    def total(f, r):
        y = Y[f, r]
        return shift_down(y[:, :ch]) + y[:, ch : 2 * ch] + shift_up(y[:, 2 * ch :])

    def finish(s, spread):
        def step(i, c):
            f, j = i // 4, i % 4
            r = j + (j // 2) * 4 if spread else j + 2
            v = total(f, r)
            if s == 0:
                v = rms_silu(v)
            else:
                v = lat[f, r].astype(F32) + v
            X[s + 1, 2 + f, 1 + r] = v.astype(BF)
            return c

        lax.fori_loop(0, 8, step, 0)

    send_outer(0)
    send_inner(0)

    ws_copy.wait()
    co = ws.shape[3]
    wsp[...] = jnp.zeros(wsp.shape, BF)
    for p, half, bs in ((0, 0, (0,)), (0, 1, (1, 2)), (1, 0, (0, 1)), (1, 1, (2,))):
        es = []
        for e in range(3):
            v = ws[bs[0], e].astype(F32)
            for b in bs[1:]:
                v = v + ws[b, e].astype(F32)
            es.append(v)
        rows = pl.ds(half * ch, ch)
        wsp[p, rows, 0:co] = (es[0] + es[1] + es[2]).astype(BF)
        wsp[p, rows, 256 : 256 + co] = es[0].astype(BF)
        wsp[p, rows, 512 : 512 + co] = es[2].astype(BF)

    for s in range(2):
        wait_w(s, 2)
        wait_w(s, 1)
        own(s, INNER)
        wait_own_halo(s)
        forward(s)
        own(s, OUTER)
        wait_w(s, 0)
        wait_outer(s)
        earlier(s, OUTER)
        finish(s, True)
        send_outer(s + 1)
        wait_inner(s)
        earlier(s, INNER)
        finish(s, False)
        send_inner(s + 1)

    wt_copy.wait()
    wait_own_halo(2)
    forward(2)

    def double(spans):
        parts = []
        for a in range(3):
            rows = []
            for f in range(2):
                for r, n in spans:
                    rows.append(X[2, f + a, r : r + n].reshape(n * wide, ch))
            parts.append(jnp.concatenate(rows, axis=0))
        lhs = jnp.concatenate(parts, axis=1)
        rhs = jnp.concatenate([wt[a] for a in range(3)], axis=0)
        d = jnp.dot(lhs, rhs, preferred_element_type=F32).astype(BF)
        at = 0
        for f in range(2):
            for r, n in spans:
                for j in range(2):
                    U[2 * f + j, r : r + n] = d[at : at + n * wide, j * ch : (j + 1) * ch].reshape(n, wide, ch)
                at += n * wide

    def space(spans, spread):
        for p in range(2):
            for f in range(4):
                parts = []
                for h in range(2):
                    rows = [U[f, r + p + h : r + p + h + n].reshape(n * wide, ch) for r, n in spans]
                    parts.append(jnp.concatenate(rows, axis=0))
                lhs = jnp.concatenate(parts, axis=1)
                d = jnp.dot(lhs, wsp[p], preferred_element_type=F32)
                Z[f] = d.reshape(4, wide, 768)

            def step(i, c):
                f, j = i // 4, i % 4
                r = j + (j // 2) * 4 if spread else j + 2
                z = Z[f, j]
                mid, left, right = z[:, :256], z[:, 256:512], z[:, 512:]
                even = mid - left + shift_down(left)
                odd = mid - right + shift_up(right)
                for h in range(2):
                    T[h, pl.ds(0, wide, stride=2), :] = even[:, h * 128 : (h + 1) * 128]
                    T[h, pl.ds(1, wide, stride=2), :] = odd[:, h * 128 : (h + 1) * 128]
                O[f, 2 * r + p, :, 0:128] = T[0].astype(BF)
                O[f, 2 * r + p, :, 128:co] = T[1, :, 0 : co - 128].astype(BF)
                return c

            lax.fori_loop(0, 16, step, 0)

    def out_copy(k):
        row, n = ((0, 4), (12, 4), (4, 8))[k]
        return pltpu.make_async_copy(
            O.at[:, pl.ds(row, n)], out.at[:, pl.ds(row, n)], out_sem.at[k]
        )

    wait_outer(2)
    double(((0, 4), (6, 4)))
    space(OUTER, True)
    out_copy(0).start()
    out_copy(1).start()
    wait_inner(2)
    double(((4, 2),))
    space(INNER, False)
    out_copy(2).start()

    for s in range(3):
        @pl.when(has_next)
        def _():
            for k in range(NY):
                y_copy(s, k).wait_send()

        @pl.when(has_up)
        def _():
            t_copy(s, 0).wait_send()

            @pl.when(has_prev)
            def _():
                t_copy(s, 2).wait_send()

        @pl.when(has_down)
        def _():
            t_copy(s, 1).wait_send()

            @pl.when(has_prev)
            def _():
                t_copy(s, 3).wait_send()

    for k in range(3):
        out_copy(k).wait()


def solution(mesh):
    tiles, groups = mesh.shape["tile"], mesh.shape["group"]

    def local(latent, conv_first, conv_second, time_weight, space_weight):
        frames, rows, wide, ch = latent.shape
        co = space_weight.shape[3]
        hbm = pl.BlockSpec(memory_space=pltpu.HBM)
        dma = pltpu.SemaphoreType.DMA
        return pl.pallas_call(
            functools.partial(kernel, tiles, groups),
            name="block",
            out_shape=jax.ShapeDtypeStruct((2 * frames, 2 * rows, 2 * wide, co), BF),
            in_specs=[hbm] * 5,
            out_specs=hbm,
            scratch_shapes=[
                pltpu.VMEM((2, 8, wide, ch), BF),
                pltpu.VMEM((3, 4, 10, wide, ch), BF),
                pltpu.VMEM((2, 3, 3, 3, ch, ch), BF),
                pltpu.VMEM((3, ch, 2 * ch), BF),
                pltpu.VMEM((3, 3, ch, co), BF),
                pltpu.VMEM((2, 2 * ch, 768), BF),
                pltpu.VMEM((2, 8, wide, 3 * ch), F32),
                pltpu.VMEM((4, 10, wide, ch), BF),
                pltpu.VMEM((4, 4, wide, 768), F32),
                pltpu.VMEM((2, 2 * wide, 128), F32),
                pltpu.VMEM((4, 16, 2 * wide, co), BF),
                dma,
                dma((2, 3, 3)),
                dma,
                dma,
                dma((3,)),
                dma((3, NY)),
                dma((3, NY)),
                dma((3, 4)),
                dma((3, 4)),
            ],
            compiler_params=pltpu.CompilerParams(
                collective_id=0, has_side_effects=True, vmem_limit_bytes=60 * 2**20
            ),
        )(latent, conv_first, conv_second, time_weight, space_weight)

    return jax.shard_map(
        local,
        mesh=mesh,
        in_specs=(P("group", "tile", None, None), P(), P(), P(), P()),
        out_specs=P("group", "tile", None, None),
        check_vma=False,
    )
```

time: 165 us -> 58.4 us (0.35)
  the two profiles are of different devices: /device:TPU:23 before, /device:TPU:60 now
where the time goes in v1:
time: 58.4 us; the launch traced here: 58.2 us
  Pallas kernels  51.2 us (88%)
  local copies, waits for them, and re-layouts  7.03 us (12%)
    pallas_call x1, Pallas kernels, local(): pl.pallas_call(functools.partial(kernel, tiles, groups), name='block', ou...  51.2 us
    unnamed x2, local copies, waits for them, and re-layouts  7.03 us

profile of v1, /device:TPU:60, one launch (start us, length us, event | category | flops | bytes accessed | tf_op | source)
XLA Modules:
  0.0 58.2 jit_solution(6818064255897221861)
XLA Ops:
  0.0 3.6 %copy.6.space_weight = bf16[3,3,384,192]{3,2,1,0:T(8,128)(2,1)} copy(bf16[3,3,384,192]{2,3,1,0:T(8,128)(2,1)} %param.9) | data formatting | bytes 2654208 | tf_op args[4]
  3.6 51.2 %block.1 = bf16[4,16,80,192]{3,2,1,0:T(8,128)(2,1)} custom-call(bf16[2,8,40,384]{3,2,1,0:T(8,128)(2,1)} %latent.1, bf16[3,3,3,384,384]{4,3,2,1,0:T(8,128)(2,1)} %conv_first.1, bf16[3,3,3,384,384]{4,3,2,1,0:T(8,128)(2,1)} %conv_second.1, bf16[3,384,768]{2,1,0:T(8,128)(2,1)} %time_weight.1, bf16[3,3,384,192]{3,2,1,0:T(8,128)(2,1)} %copy.6.space_weight), custom_call_target="tpu_custom_call" | custom-call | tf_op jit(solution)/shard_map/block/pallas_call | solution.py:379
  54.8 3.4 %copy.8 = bf16[4,16,80,192]{3,2,1,0:T(8,128)(2,1)} copy(bf16[4,16,80,192]{3,2,1,0:T(8,128)(2,1)} %block.1) | data formatting | bytes 3932160

commit v2 on v1

--- a/solution.py
+++ b/solution.py
@@ -37,8 +37,8 @@
 def kernel(
     tiles, groups,
     latent, conv_first, conv_second, time_weight, space_weight, out,
-    lat, X, W, wt, ws, wsp, Y, U, Z, T, O,
-    lat_sem, w_sem, wt_sem, ws_sem, out_sem, y_send, y_recv, t_send, t_recv,
+    lat, X, W, wt, ws, wsp, Y, U, Z, T,
+    lat_sem, w_sem, wt_sem, ws_sem, y_send, y_recv, t_send, t_recv,
 ):
     t = lax.axis_index("tile")
     g = lax.axis_index("group")
@@ -98,7 +98,7 @@
         X[0, 2 + f, 1 + r] = rms_silu(lat[f, r].astype(F32)).astype(BF)
         return c
 
-    lax.fori_loop(0, 16, act_own, 0)
+    lax.fori_loop(0, 16, act_own, 0, unroll=4)
 
     pl.semaphore_wait(barrier, 4)
 
@@ -240,14 +240,16 @@
             X[s + 1, 2 + f, 1 + r] = v.astype(BF)
             return c
 
-        lax.fori_loop(0, 8, step, 0)
+        lax.fori_loop(0, 8, step, 0, unroll=4)
 
     send_outer(0)
     send_inner(0)
 
     ws_copy.wait()
-    co = ws.shape[3]
-    wsp[...] = jnp.zeros(wsp.shape, BF)
+    co = ws.shape[2]
+    for p in range(2):
+        for k in range(3):
+            wsp[p, :, 256 * k + co : 256 * (k + 1)] = jnp.zeros((2 * ch, 256 - co), BF)
     for p, half, bs in ((0, 0, (0,)), (0, 1, (1, 2)), (1, 0, (0, 1)), (1, 1, (2,))):
         es = []
         for e in range(3):
@@ -256,9 +258,8 @@
                 v = v + ws[b, e].astype(F32)
             es.append(v)
         rows = pl.ds(half * ch, ch)
-        wsp[p, rows, 0:co] = (es[0] + es[1] + es[2]).astype(BF)
-        wsp[p, rows, 256 : 256 + co] = es[0].astype(BF)
-        wsp[p, rows, 512 : 512 + co] = es[2].astype(BF)
+        for k, v in enumerate((es[0] + es[1] + es[2], es[0], es[2])):
+            wsp[p, rows, 256 * k : 256 * k + co] = v.T.astype(BF)
 
     for s in range(2):
         wait_w(s, 2)
@@ -299,48 +300,45 @@
                     U[2 * f + j, r : r + n] = d[at : at + n * wide, j * ch : (j + 1) * ch].reshape(n, wide, ch)
                 at += n * wide
 
-    def space(spans, spread):
-        for p in range(2):
-            for f in range(4):
-                parts = []
-                for h in range(2):
-                    rows = [U[f, r + p + h : r + p + h + n].reshape(n * wide, ch) for r, n in spans]
-                    parts.append(jnp.concatenate(rows, axis=0))
-                lhs = jnp.concatenate(parts, axis=1)
-                d = jnp.dot(lhs, wsp[p], preferred_element_type=F32)
-                Z[f] = d.reshape(4, wide, 768)
-
-            def step(i, c):
-                f, j = i // 4, i % 4
-                r = j + (j // 2) * 4 if spread else j + 2
+    def space(spans):
+        rows_of = [r + k for r, n in spans for k in range(n)]
+
+        def product(unit):
+            p, f = unit
+            parts = []
+            for h in range(2):
+                rows = [U[f, r + p + h : r + p + h + n].reshape(n * wide, ch) for r, n in spans]
+                parts.append(jnp.concatenate(rows, axis=0))
+            lhs = jnp.concatenate(parts, axis=1)
+            d = jnp.dot(lhs, wsp[p], preferred_element_type=F32)
+            Z[f] = d.reshape(4, wide, 768)
+
+        def spread_columns(unit):
+            p, f = unit
+            for j, r in enumerate(rows_of):
                 z = Z[f, j]
                 mid, left, right = z[:, :256], z[:, 256:512], z[:, 512:]
                 even = mid - left + shift_down(left)
                 odd = mid - right + shift_up(right)
                 for h in range(2):
-                    T[h, pl.ds(0, wide, stride=2), :] = even[:, h * 128 : (h + 1) * 128]
-                    T[h, pl.ds(1, wide, stride=2), :] = odd[:, h * 128 : (h + 1) * 128]
-                O[f, 2 * r + p, :, 0:128] = T[0].astype(BF)
-                O[f, 2 * r + p, :, 128:co] = T[1, :, 0 : co - 128].astype(BF)
-                return c
-
-            lax.fori_loop(0, 16, step, 0)
-
-    def out_copy(k):
-        row, n = ((0, 4), (12, 4), (4, 8))[k]
-        return pltpu.make_async_copy(
-            O.at[:, pl.ds(row, n)], out.at[:, pl.ds(row, n)], out_sem.at[k]
-        )
+                    T[j, h, pl.ds(0, wide, stride=2), :] = even[:, h * 128 : (h + 1) * 128]
+                    T[j, h, pl.ds(1, wide, stride=2), :] = odd[:, h * 128 : (h + 1) * 128]
+                out[f, 2 * r + p, :, 0:128] = T[j, 0].astype(BF)
+                out[f, 2 * r + p, :, 128:co] = T[j, 1, :, 0 : co - 128].astype(BF)
+
+        units = [(p, f) for p in range(2) for f in range(4)]
+        product(units[0])
+        for k in range(1, len(units)):
+            product(units[k])
+            spread_columns(units[k - 1])
+        spread_columns(units[-1])
 
     wait_outer(2)
     double(((0, 4), (6, 4)))
-    space(OUTER, True)
-    out_copy(0).start()
-    out_copy(1).start()
+    space(OUTER)
     wait_inner(2)
     double(((4, 2),))
-    space(INNER, False)
-    out_copy(2).start()
+    space(INNER)
 
     for s in range(3):
         @pl.when(has_next)
@@ -363,9 +361,6 @@
             @pl.when(has_prev)
             def _():
                 t_copy(s, 3).wait_send()
-
-    for k in range(3):
-        out_copy(k).wait()
 
 
 def solution(mesh):
@@ -379,35 +374,33 @@
         return pl.pallas_call(
             functools.partial(kernel, tiles, groups),
             name="block",
-            out_shape=jax.ShapeDtypeStruct((2 * frames, 2 * rows, 2 * wide, co), BF),
+            out_shape=pltpu.VMEM((2 * frames, 2 * rows, 2 * wide, co), BF),
             in_specs=[hbm] * 5,
-            out_specs=hbm,
+            out_specs=pl.BlockSpec(memory_space=pltpu.VMEM),
             scratch_shapes=[
                 pltpu.VMEM((2, 8, wide, ch), BF),
                 pltpu.VMEM((3, 4, 10, wide, ch), BF),
                 pltpu.VMEM((2, 3, 3, 3, ch, ch), BF),
                 pltpu.VMEM((3, ch, 2 * ch), BF),
-                pltpu.VMEM((3, 3, ch, co), BF),
+                pltpu.VMEM((3, 3, co, ch), BF),
                 pltpu.VMEM((2, 2 * ch, 768), BF),
                 pltpu.VMEM((2, 8, wide, 3 * ch), F32),
                 pltpu.VMEM((4, 10, wide, ch), BF),
                 pltpu.VMEM((4, 4, wide, 768), F32),
-                pltpu.VMEM((2, 2 * wide, 128), F32),
-                pltpu.VMEM((4, 16, 2 * wide, co), BF),
+                pltpu.VMEM((4, 2, 2 * wide, 128), F32),
                 dma,
                 dma((2, 3, 3)),
                 dma,
                 dma,
-                dma((3,)),
                 dma((3, NY)),
                 dma((3, NY)),
                 dma((3, 4)),
                 dma((3, 4)),
             ],
             compiler_params=pltpu.CompilerParams(
-                collective_id=0, has_side_effects=True, vmem_limit_bytes=60 * 2**20
+                collective_id=0, has_side_effects=True, vmem_limit_bytes=51 * 2**20
             ),
-        )(latent, conv_first, conv_second, time_weight, space_weight)
+        )(latent, conv_first, conv_second, time_weight, jnp.swapaxes(space_weight, 2, 3))
 
     return jax.shard_map(
         local,

time: 58.4 us -> 48 us (0.82)
  local copies, waits for them, and re-layouts: 7.03 us -> 1.49 us
  Pallas kernels: 51.2 us -> 46.1 us
    unnamed x2 -> x1, local copies, waits for them, and re-layouts: 7.03 us -> 1.49 us
    pallas_call x1, Pallas kernels: 51.2 us -> 46.1 us  [local(): pl.pallas_call(functools.partial(kernel, tiles, groups), name='block', ou...]
where the time goes in v2:
time: 48 us; the launch traced here: 47.6 us
  Pallas kernels  46.1 us (96%)
  local copies, waits for them, and re-layouts  1.49 us (3%)
    pallas_call x1, Pallas kernels, local(): pl.pallas_call(functools.partial(kernel, tiles, groups), name='block', ou...  46.1 us
    unnamed x1, local copies, waits for them, and re-layouts  1.49 us

profile of v2, /device:TPU:60, one launch (start us, length us, event | category | flops | bytes accessed | tf_op | source)
XLA Modules:
  0.0 47.6 jit_solution(585749884751831312)
XLA Ops:
  0.0 46.1 %block.1 = bf16[4,16,80,192]{3,2,1,0:T(8,128)(2,1)S(1)} custom-call(bf16[2,8,40,384]{3,2,1,0:T(8,128)(2,1)} %latent.1, bf16[3,3,3,384,384]{4,3,2,1,0:T(8,128)(2,1)} %conv_first.1, bf16[3,3,3,384,384]{4,3,2,1,0:T(8,128)(2,1)} %conv_second.1, bf16[3,384,768]{2,1,0:T(8,128)(2,1)} %time_weight.1, bf16[3,3,192,384]{3,2,1,0:T(8,128)(2,1)} %bitcast.1), custom_call_target="tpu_custom_call" | custom-call | tf_op jit(solution)/shard_map/block/pallas_call | solution.py:374
  46.1 1.5 %copy.7 = bf16[4,16,80,192]{3,2,1,0:T(8,128)(2,1)} copy(bf16[4,16,80,192]{3,2,1,0:T(8,128)(2,1)S(1)} %block.1) | data formatting | bytes 3932160

commit v3 on v2

--- a/solution.py
+++ b/solution.py
@@ -12,10 +12,10 @@
 F32 = jnp.float32
 
 OUTER = ((0, 2), (6, 2))
+EDGES = ((0, 1), (7, 1))
+MIDDLE = ((1, 1), (6, 1))
 INNER = ((2, 4),)
-OUTER_SENDS = ((1, 1), (8, 1), (2, 1), (7, 1))
-INNER_SENDS = ((3, 1), (6, 1), (4, 2))
-SENDS = OUTER_SENDS + INNER_SENDS
+SENDS = ((1, 1), (8, 1), (2, 1), (7, 1), (3, 1), (6, 1), (4, 2))
 NY = len(SENDS)
 
 
@@ -44,6 +44,7 @@
     g = lax.axis_index("group")
     wide = lat.shape[2]
     ch = lat.shape[3]
+    co = ws.shape[2]
     has_up, has_down = t > 0, t < tiles - 1
     has_prev, has_next = g > 0, g < groups - 1
     up = (lax.rem(t + tiles - 1, tiles), g)
@@ -62,14 +63,10 @@
         for a in (2, 1, 0):
             for b in range(3):
                 w_copies.append(pltpu.make_async_copy(src.at[a, b], W.at[s, a, b], w_sem.at[s, a, b]))
-    for c in w_copies[:9]:
+    for c in w_copies[:6]:
         c.start()
     wt_copy = pltpu.make_async_copy(time_weight, wt, wt_sem)
     ws_copy = pltpu.make_async_copy(space_weight, ws, ws_sem)
-    ws_copy.start()
-    for c in w_copies[9:]:
-        c.start()
-    wt_copy.start()
 
     def wait_w(s, a):
         for b in range(3):
@@ -125,7 +122,7 @@
             device_id_type=MESH,
         )
 
-    def send_outer(s):
+    def send_edges(s):
         @pl.when(has_next)
         def _():
             y_copy(s, 0).start()
@@ -139,6 +136,7 @@
         def _():
             t_copy(s, 1).start()
 
+    def send_middle(s):
         @pl.when(has_next)
         def _():
             y_copy(s, 2).start()
@@ -147,7 +145,7 @@
     def send_inner(s):
         @pl.when(has_next)
         def _():
-            for k in range(len(OUTER_SENDS), NY):
+            for k in range(4, NY):
                 y_copy(s, k).start()
 
     def wait_own_halo(s):
@@ -174,11 +172,11 @@
             def _():
                 t_copy(s, 3).start()
 
-    def wait_outer(s):
+    def wait_edges(s):
         @pl.when(has_prev)
         def _():
-            for k in range(2, NY - 1):
-                y_copy(s, k).wait_recv()
+            y_copy(s, 2).wait_recv()
+            y_copy(s, 3).wait_recv()
 
             @pl.when(has_down)
             def _():
@@ -187,6 +185,12 @@
             @pl.when(has_up)
             def _():
                 t_copy(s, 3).wait_recv()
+
+    def wait_middle(s):
+        @pl.when(has_prev)
+        def _():
+            y_copy(s, 4).wait_recv()
+            y_copy(s, 5).wait_recv()
 
     def wait_inner(s):
         @pl.when(has_prev)
@@ -216,22 +220,61 @@
                     Y[f, r : r + n] += piece
                 at += n * wide
 
+    def sum_taps():
+        ws_copy.wait()
+        for p in range(2):
+            for k in range(3):
+                wsp[p, :, 256 * k + co : 256 * (k + 1)] = jnp.zeros((2 * ch, 256 - co), BF)
+        for p, half, bs in ((0, 0, (0,)), (0, 1, (1, 2)), (1, 0, (0, 1)), (1, 1, (2,))):
+            es = []
+            for e in range(3):
+                v = ws[bs[0], e].astype(F32)
+                for b in bs[1:]:
+                    v = v + ws[b, e].astype(F32)
+                es.append(v)
+            rows = pl.ds(half * ch, ch)
+            for k, v in enumerate((es[0] + es[1] + es[2], es[0], es[2])):
+                wsp[p, rows, 256 * k : 256 * k + co] = v.T.astype(BF)
+
+    def joined(s, f, steps, spans, first):
+        parts = []
+        for a in steps:
+            for b in range(3):
+                rows = [X[s, f + a, r + b : r + b + n].reshape(n * wide, ch) for r, n in spans]
+                parts.append(jnp.concatenate(rows, axis=0))
+        lhs = jnp.concatenate(parts, axis=1)
+        rhs = jnp.concatenate(
+            [jnp.concatenate([W[s, a, b, e] for e in range(3)], axis=1) for a in steps for b in range(3)], axis=0
+        )
+        d = jnp.dot(lhs, rhs, preferred_element_type=F32)
+        at = 0
+        for r, n in spans:
+            piece = d[at : at + n * wide].reshape(n, wide, 3 * ch)
+            if first:
+                Y[f, r : r + n] = piece
+            else:
+                Y[f, r : r + n] += piece
+            at += n * wide
+
     def own(s, spans):
-        taps(s, 2, (0, 1), spans, True)
-        taps(s, 1, (1,), spans, False)
-
-    def earlier(s, spans):
+        joined(s, 1, (1, 2), spans, True)
+        joined(s, 0, (2,), spans, True)
+
+    def earlier_small(s, spans):
         taps(s, 1, (0,), spans, False)
         taps(s, 0, (0, 1), spans, False)
+
+    def earlier(s, spans):
+        joined(s, 0, (0, 1), spans, False)
+        joined(s, 1, (0,), spans, False)
 
     def total(f, r):
         y = Y[f, r]
         return shift_down(y[:, :ch]) + y[:, ch : 2 * ch] + shift_up(y[:, 2 * ch :])
 
-    def finish(s, spread):
-        def step(i, c):
-            f, j = i // 4, i % 4
-            r = j + (j // 2) * 4 if spread else j + 2
+    def finish(s, start, step, count):
+        def one(i, c):
+            f, r = i // count, start + step * (i % count)
             v = total(f, r)
             if s == 0:
                 v = rms_silu(v)
@@ -240,26 +283,13 @@
             X[s + 1, 2 + f, 1 + r] = v.astype(BF)
             return c
 
-        lax.fori_loop(0, 8, step, 0, unroll=4)
-
-    send_outer(0)
+        lax.fori_loop(0, 2 * count, one, 0, unroll=4)
+
+    send_edges(0)
+    send_middle(0)
     send_inner(0)
-
-    ws_copy.wait()
-    co = ws.shape[2]
-    for p in range(2):
-        for k in range(3):
-            wsp[p, :, 256 * k + co : 256 * (k + 1)] = jnp.zeros((2 * ch, 256 - co), BF)
-    for p, half, bs in ((0, 0, (0,)), (0, 1, (1, 2)), (1, 0, (0, 1)), (1, 1, (2,))):
-        es = []
-        for e in range(3):
-            v = ws[bs[0], e].astype(F32)
-            for b in bs[1:]:
-                v = v + ws[b, e].astype(F32)
-            es.append(v)
-        rows = pl.ds(half * ch, ch)
-        for k, v in enumerate((es[0] + es[1] + es[2], es[0], es[2])):
-            wsp[p, rows, 256 * k : 256 * k + co] = v.T.astype(BF)
+    for c in w_copies[6:] + [ws_copy, wt_copy]:
+        c.start()
 
     for s in range(2):
         wait_w(s, 2)
@@ -269,15 +299,20 @@
         forward(s)
         own(s, OUTER)
         wait_w(s, 0)
-        wait_outer(s)
-        earlier(s, OUTER)
-        finish(s, True)
-        send_outer(s + 1)
+        wait_edges(s)
+        earlier_small(s, EDGES)
+        finish(s, 0, 7, 2)
+        send_edges(s + 1)
+        wait_middle(s)
+        earlier_small(s, MIDDLE)
+        finish(s, 1, 5, 2)
+        send_middle(s + 1)
         wait_inner(s)
         earlier(s, INNER)
-        finish(s, False)
+        finish(s, 2, 1, 4)
         send_inner(s + 1)
 
+    sum_taps()
     wt_copy.wait()
     wait_own_halo(2)
     forward(2)
@@ -333,7 +368,8 @@
             spread_columns(units[k - 1])
         spread_columns(units[-1])
 
-    wait_outer(2)
+    wait_edges(2)
+    wait_middle(2)
     double(((0, 4), (6, 4)))
     space(OUTER)
     wait_inner(2)

time: 48 us -> 43 us (0.90)
  the two profiles are of different devices: /device:TPU:60 before, /device:TPU:16 now
where the time goes in v3:
time: 43 us; the launch traced here: 42.9 us
  Pallas kernels  41.4 us (96%)
  local copies, waits for them, and re-layouts  1.49 us (3%)
    pallas_call x1, Pallas kernels, local(): pl.pallas_call(functools.partial(kernel, tiles, groups), name='block', ou...  41.4 us
    unnamed x1, local copies, waits for them, and re-layouts  1.49 us

profile of v3, /device:TPU:16, one launch (start us, length us, event | category | flops | bytes accessed | tf_op | source)
XLA Modules:
  0.0 42.9 jit_solution(3582037127380043163)
XLA Ops:
  0.0 41.4 %block.1 = bf16[4,16,80,192]{3,2,1,0:T(8,128)(2,1)S(1)} custom-call(bf16[2,8,40,384]{3,2,1,0:T(8,128)(2,1)} %latent.1, bf16[3,3,3,384,384]{4,3,2,1,0:T(8,128)(2,1)} %conv_first.1, bf16[3,3,3,384,384]{4,3,2,1,0:T(8,128)(2,1)} %conv_second.1, bf16[3,384,768]{2,1,0:T(8,128)(2,1)} %time_weight.1, bf16[3,3,192,384]{3,2,1,0:T(8,128)(2,1)} %bitcast.1), custom_call_target="tpu_custom_call" | custom-call | tf_op jit(solution)/shard_map/block/pallas_call | solution.py:410
  41.4 1.5 %copy.7 = bf16[4,16,80,192]{3,2,1,0:T(8,128)(2,1)} copy(bf16[4,16,80,192]{3,2,1,0:T(8,128)(2,1)S(1)} %block.1) | data formatting | bytes 3932160

commit v4 on v3

--- a/solution.py
+++ b/solution.py
@@ -37,7 +37,7 @@
 def kernel(
     tiles, groups,
     latent, conv_first, conv_second, time_weight, space_weight, out,
-    lat, X, W, wt, ws, wsp, Y, U, Z, T,
+    lat, X, W, wt, ws, wsp, Y, D, U, Z, T,
     lat_sem, w_sem, wt_sem, ws_sem, y_send, y_recv, t_send, t_recv,
 ):
     t = lax.axis_index("tile")
@@ -123,18 +123,18 @@
         )
 
     def send_edges(s):
+        @pl.when(has_up)
+        def _():
+            t_copy(s, 0).start()
+
+        @pl.when(has_down)
+        def _():
+            t_copy(s, 1).start()
+
         @pl.when(has_next)
         def _():
             y_copy(s, 0).start()
             y_copy(s, 1).start()
-
-        @pl.when(has_up)
-        def _():
-            t_copy(s, 0).start()
-
-        @pl.when(has_down)
-        def _():
-            t_copy(s, 1).start()
 
     def send_middle(s):
         @pl.when(has_next)
@@ -294,9 +294,13 @@
     for s in range(2):
         wait_w(s, 2)
         wait_w(s, 1)
-        own(s, INNER)
+        if s == 0:
+            own(s, INNER)
+            forward(s)
+        else:
+            forward(s)
+            own(s, INNER)
         wait_own_halo(s)
-        forward(s)
         own(s, OUTER)
         wait_w(s, 0)
         wait_edges(s)
@@ -312,27 +316,28 @@
         finish(s, 2, 1, 4)
         send_inner(s + 1)
 
+    forward(2)
     sum_taps()
     wt_copy.wait()
     wait_own_halo(2)
-    forward(2)
-
-    def double(spans):
+
+    def time_product(f, steps, spans):
         parts = []
-        for a in range(3):
-            rows = []
-            for f in range(2):
-                for r, n in spans:
-                    rows.append(X[2, f + a, r : r + n].reshape(n * wide, ch))
+        for a in steps:
+            rows = [X[2, f + a, r : r + n].reshape(n * wide, ch) for r, n in spans]
             parts.append(jnp.concatenate(rows, axis=0))
         lhs = jnp.concatenate(parts, axis=1)
-        rhs = jnp.concatenate([wt[a] for a in range(3)], axis=0)
-        d = jnp.dot(lhs, rhs, preferred_element_type=F32).astype(BF)
-        at = 0
-        for f in range(2):
+        rhs = jnp.concatenate([wt[a] for a in steps], axis=0)
+        return jnp.dot(lhs, rhs, preferred_element_type=F32)
+
+    def double(spans):
+        for f, steps in ((0, (0, 1)), (1, (0,))):
+            d = time_product(f, steps, spans)
+            at = 0
             for r, n in spans:
+                v = (d[at : at + n * wide].reshape(n, wide, 2 * ch) + D[f, r : r + n]).astype(BF)
                 for j in range(2):
-                    U[2 * f + j, r : r + n] = d[at : at + n * wide, j * ch : (j + 1) * ch].reshape(n, wide, ch)
+                    U[2 * f + j, r : r + n] = v[:, :, j * ch : (j + 1) * ch]
                 at += n * wide
 
     def space(spans):
@@ -368,6 +373,8 @@
             spread_columns(units[k - 1])
         spread_columns(units[-1])
 
+    D[0] = time_product(0, (2,), ((0, 10),)).reshape(10, wide, 2 * ch)
+    D[1] = time_product(1, (1, 2), ((0, 10),)).reshape(10, wide, 2 * ch)
     wait_edges(2)
     wait_middle(2)
     double(((0, 4), (6, 4)))
@@ -421,6 +428,7 @@
                 pltpu.VMEM((3, 3, co, ch), BF),
                 pltpu.VMEM((2, 2 * ch, 768), BF),
                 pltpu.VMEM((2, 8, wide, 3 * ch), F32),
+                pltpu.VMEM((2, 10, wide, 2 * ch), F32),
                 pltpu.VMEM((4, 10, wide, ch), BF),
                 pltpu.VMEM((4, 4, wide, 768), F32),
                 pltpu.VMEM((4, 2, 2 * wide, 128), F32),

time: 43 us -> 42 us (0.977)
  the two profiles are of different devices: /device:TPU:16 before, /device:TPU:60 now
where the time goes in v4:
time: 42 us; the launch traced here: 41.7 us
  Pallas kernels  40.2 us (96%)
  local copies, waits for them, and re-layouts  1.49 us (4%)
    pallas_call x1, Pallas kernels, local(): pl.pallas_call(functools.partial(kernel, tiles, groups), name='block', ou...  40.2 us
    unnamed x1, local copies, waits for them, and re-layouts  1.49 us

profile of v4, /device:TPU:60, one launch (start us, length us, event | category | flops | bytes accessed | tf_op | source)
XLA Modules:
  0.0 41.7 jit_solution(4208725202909361722)
XLA Ops:
  0.0 40.2 %block.1 = bf16[4,16,80,192]{3,2,1,0:T(8,128)(2,1)S(1)} custom-call(bf16[2,8,40,384]{3,2,1,0:T(8,128)(2,1)} %latent.1, bf16[3,3,3,384,384]{4,3,2,1,0:T(8,128)(2,1)} %conv_first.1, bf16[3,3,3,384,384]{4,3,2,1,0:T(8,128)(2,1)} %conv_second.1, bf16[3,384,768]{2,1,0:T(8,128)(2,1)} %time_weight.1, bf16[3,3,192,384]{3,2,1,0:T(8,128)(2,1)} %bitcast.1), custom_call_target="tpu_custom_call" | custom-call | tf_op jit(solution)/shard_map/block/pallas_call | solution.py:417
  40.2 1.5 %copy.7 = bf16[4,16,80,192]{3,2,1,0:T(8,128)(2,1)} copy(bf16[4,16,80,192]{3,2,1,0:T(8,128)(2,1)S(1)} %block.1) | data formatting | bytes 3932160

commit v5 on v4

--- a/solution.py
+++ b/solution.py
@@ -288,7 +288,7 @@
     send_edges(0)
     send_middle(0)
     send_inner(0)
-    for c in w_copies[6:] + [ws_copy, wt_copy]:
+    for c in w_copies[6:15]:
         c.start()
 
     for s in range(2):
@@ -311,10 +311,16 @@
         earlier_small(s, MIDDLE)
         finish(s, 1, 5, 2)
         send_middle(s + 1)
+        if s == 0:
+            for c in w_copies[15:]:
+                c.start()
         wait_inner(s)
         earlier(s, INNER)
         finish(s, 2, 1, 4)
         send_inner(s + 1)
+        if s == 0:
+            ws_copy.start()
+            wt_copy.start()
 
     forward(2)
     sum_taps()

time: 42 us -> 42 us (level)
  no operation moved by 1% of the time
where the time goes in v5:
time: 42 us; the launch traced here: 41.7 us
  Pallas kernels  40.2 us (96%)
  local copies, waits for them, and re-layouts  1.49 us (4%)
    pallas_call x1, Pallas kernels, local(): pl.pallas_call(functools.partial(kernel, tiles, groups), name='block', ou...  40.2 us
    unnamed x1, local copies, waits for them, and re-layouts  1.49 us

profile of v5, /device:TPU:60, one launch (start us, length us, event | category | flops | bytes accessed | tf_op | source)
XLA Modules:
  0.0 41.7 jit_solution(5111381395988858932)
XLA Ops:
  0.0 40.2 %block.1 = bf16[4,16,80,192]{3,2,1,0:T(8,128)(2,1)S(1)} custom-call(bf16[2,8,40,384]{3,2,1,0:T(8,128)(2,1)} %latent.1, bf16[3,3,3,384,384]{4,3,2,1,0:T(8,128)(2,1)} %conv_first.1, bf16[3,3,3,384,384]{4,3,2,1,0:T(8,128)(2,1)} %conv_second.1, bf16[3,384,768]{2,1,0:T(8,128)(2,1)} %time_weight.1, bf16[3,3,192,384]{3,2,1,0:T(8,128)(2,1)} %bitcast.1), custom_call_target="tpu_custom_call" | custom-call | tf_op jit(solution)/shard_map/block/pallas_call | solution.py:423
  40.2 1.5 %copy.7 = bf16[4,16,80,192]{3,2,1,0:T(8,128)(2,1)} copy(bf16[4,16,80,192]{3,2,1,0:T(8,128)(2,1)S(1)} %block.1) | data formatting | bytes 3932160

commit v6 on v4

--- a/solution.py
+++ b/solution.py
@@ -376,8 +376,9 @@
     D[0] = time_product(0, (2,), ((0, 10),)).reshape(10, wide, 2 * ch)
     D[1] = time_product(1, (1, 2), ((0, 10),)).reshape(10, wide, 2 * ch)
     wait_edges(2)
+    double(((0, 3), (7, 3)))
     wait_middle(2)
-    double(((0, 4), (6, 4)))
+    double(((3, 1), (6, 1)))
     space(OUTER)
     wait_inner(2)
     double(((4, 2),))

time: 42 us -> 41.4 us (0.986)
  Pallas kernels: 40.2 us -> 39.6 us
    pallas_call x1, Pallas kernels: 40.2 us -> 39.6 us  [local(): pl.pallas_call(functools.partial(kernel, tiles, groups), name='block', ou...]
where the time goes in v6:
time: 41.4 us; the launch traced here: 41.1 us
  Pallas kernels  39.6 us (96%)
  local copies, waits for them, and re-layouts  1.49 us (4%)
    pallas_call x1, Pallas kernels, local(): pl.pallas_call(functools.partial(kernel, tiles, groups), name='block', ou...  39.6 us
    unnamed x1, local copies, waits for them, and re-layouts  1.49 us

profile of v6, /device:TPU:60, one launch (start us, length us, event | category | flops | bytes accessed | tf_op | source)
XLA Modules:
  0.0 41.1 jit_solution(4515190967949908695)
XLA Ops:
  0.0 39.6 %block.1 = bf16[4,16,80,192]{3,2,1,0:T(8,128)(2,1)S(1)} custom-call(bf16[2,8,40,384]{3,2,1,0:T(8,128)(2,1)} %latent.1, bf16[3,3,3,384,384]{4,3,2,1,0:T(8,128)(2,1)} %conv_first.1, bf16[3,3,3,384,384]{4,3,2,1,0:T(8,128)(2,1)} %conv_second.1, bf16[3,384,768]{2,1,0:T(8,128)(2,1)} %time_weight.1, bf16[3,3,192,384]{3,2,1,0:T(8,128)(2,1)} %bitcast.1), custom_call_target="tpu_custom_call" | custom-call | tf_op jit(solution)/shard_map/block/pallas_call | solution.py:418
  39.6 1.5 %copy.7 = bf16[4,16,80,192]{3,2,1,0:T(8,128)(2,1)} copy(bf16[4,16,80,192]{3,2,1,0:T(8,128)(2,1)S(1)} %block.1) | data formatting | bytes 3932160
